TPU v7x, 32 devices: a whole 2x2x4 slice. The times are simulated.
32 devices in a mesh: section: 4 (over y, core), dp: 4 (over z), tensor: 2 (over x).
Axes of the slice: x: 2, y: 2, z: 4, core: 2. Of those that a mesh axis runs over, the one named last changes fastest.
Arguments:
- hidden_in: bfloat16 [1024, 5120], P('dp', 'tensor'), may hold values from -6 to 6
- kv_cache: bfloat16 [4, 4, 2, 1024, 512], P('section', 'dp', None, None, 'tensor'), may hold values from -512 to 512
- norm_gain: float32 [4, 5120], P('section'), may hold values from 0.25 to 1.75
- w_query: bfloat16 [4, 5120, 2560], P('section', 'dp', 'tensor'), may hold values from -0.078125 to 0.078125
- w_keyval: bfloat16 [4, 5120, 2, 512], P('section', 'dp', None, 'tensor'), may hold values from -0.078125 to 0.078125
- w_out: bfloat16 [4, 2560, 5120], P('section', 'tensor', 'dp'), may hold values from -1.1953125 to 1.1953125
- stretch_count: int32 [4], P('dp'), may hold values from 1 to 2, 6 in all
- prefix_len: int32 [4], P('dp'), may hold values from 1 to 1024, 2560 in all
Outputs:
- attn_out: bfloat16 [4, 1024, 5120], P('section', 'dp', 'tensor')
- hidden_out: bfloat16 [4, 1024, 5120], P('section', 'dp', 'tensor')
Inputs may be any that keep to these rules, and one draw needn't show every extreme that they name: `stretch_count`: some transcript has 2 live stretches. `prefix_len`: some transcript keeps 1024 rows.
All inputs are finite; a program needn't handle non-finite values. No bound on the sum of `stretch_count` or of `prefix_len` on one device may be relied on, other than what follows from the above.
Results may differ from a plain program's by a relative error of at most 0.02.
Values may be sent and summed in bfloat16 or wider, within the bound.
A program may use at most 128 MiB of HBM per device.

v0:
```python
import jax
import jax.numpy as jnp
from jax import lax
from jax.sharding import PartitionSpec as P

HEAD_DIM = 128
STRETCH = 128


theta_base = 1000000.0
eps_norm = 1e-06
masked_score = -1e30


def from_behind(value, axis, steps):
    count = lax.axis_size(axis)
    leading, last = (max(0, -steps), min(count, count - steps))
    return lax.ppermute(value, axis, [(source, source + steps) for source in range(leading, last)])


def rotary(values, positions):
    half_dim = values.shape[-1] // 2
    inv_freq = theta_base ** (-(jnp.arange(half_dim, dtype=jnp.float32) * 2.0 / values.shape[-1]))
    angles = positions.astype(jnp.float32)[:, None] * inv_freq[None, :]
    cosine = jnp.cos(angles)[:, None, :]
    sine_part = jnp.sin(angles)[:, None, :]
    first_half = values[..., :half_dim]
    second_half = values[..., half_dim:]
    return jnp.concatenate(
        [
            first_half * cosine - second_half * sine_part,
            second_half * cosine + first_half * sine_part,
        ],
        axis=-1,
    )


def shards(hidden_in, kv_cache, norm_gain, w_query, w_keyval, w_out, stretch_count, prefix_len):
    section_idx = lax.axis_index("section")
    section_total = lax.axis_size("section")
    tensor_idx = lax.axis_index("tensor")
    query_w, keyval_w = (
        lax.all_gather(w_query, "dp", axis=1, tiled=True),
        lax.all_gather(w_keyval, "dp", axis=1, tiled=True),
    )
    out_w = lax.all_gather(w_out, "dp", axis=2, tiled=True)[0]
    query_w = query_w[0]
    width = query_w.shape[0]
    local_cols = query_w.shape[1]
    keyval_w = keyval_w[0].reshape(width, -1)
    gain_vec = norm_gain[0]
    kv_store = kv_cache[0, 0]
    live_count = stretch_count[0]
    prefix = prefix_len[0]
    rows_all = hidden_in.shape[0]
    slot_total = rows_all // STRETCH
    part_width = hidden_in.shape[1]
    kv_width = kv_store.shape[2]
    kv_local = kv_width // HEAD_DIM
    heads_local = local_cols // HEAD_DIM
    group_size = heads_local // kv_local
    prefix_cap = kv_store.shape[1]
    key_block = min(prefix_cap, 512)
    block_total = prefix_cap // key_block
    score_scale = HEAD_DIM ** (-0.5)
    tick_total = slot_total + section_total - 1
    full_prec = lax.Precision.HIGHEST
    key_buf = jnp.zeros((rows_all, kv_width), jnp.bfloat16)
    value_buf = jnp.zeros((rows_all, kv_width), jnp.bfloat16)
    attn_buf = jnp.zeros((rows_all, part_width), jnp.bfloat16)
    hid_buf = jnp.zeros((rows_all, part_width), jnp.bfloat16)
    inputs_all = lax.all_gather(hidden_in, "tensor", axis=1, tiled=True)
    incoming = jnp.zeros((STRETCH, width), jnp.bfloat16)
    for tick_num in range(tick_total):
        slot_num = tick_num - section_idx
        valid = (slot_num >= 0) & (slot_num < slot_total)
        slot_safe = jnp.clip(slot_num, 0, slot_total - 1)
        row_start = slot_safe * STRETCH
        first_rows = lax.dynamic_slice_in_dim(inputs_all, row_start, STRETCH, 0)
        x_full = jnp.where(section_idx == 0, first_rows, incoming)
        x_part = lax.dynamic_slice_in_dim(x_full, tensor_idx * part_width, part_width, 1)
        x_float = x_full.astype(jnp.float32)
        normed = (
            x_float
            * lax.rsqrt(jnp.mean(x_float * x_float, axis=1, keepdims=True) + eps_norm)
            * gain_vec[None, :]
        ).astype(jnp.bfloat16)
        positions = prefix + row_start + jnp.arange(STRETCH, dtype=jnp.int32)
        query_vec = jnp.dot(normed, query_w, preferred_element_type=jnp.float32).reshape(
            STRETCH, heads_local, HEAD_DIM
        )
        query_vec = rotary(query_vec, positions)
        keyval = jnp.dot(normed, keyval_w, preferred_element_type=jnp.float32)
        key_new = (
            rotary(keyval[:, :kv_width].reshape(STRETCH, kv_local, HEAD_DIM), positions)
            .astype(jnp.bfloat16)
            .reshape(STRETCH, kv_width)
        )
        value_new = keyval[:, kv_width:].astype(jnp.bfloat16)
        key_upd = lax.dynamic_update_slice(key_buf, key_new, (row_start, 0))
        value_upd = lax.dynamic_update_slice(value_buf, value_new, (row_start, 0))
        key_buf = jnp.where(valid, key_upd, key_buf)
        value_buf = jnp.where(valid, value_upd, value_buf)
        query_rows = (
            query_vec.reshape(STRETCH, kv_local, group_size, HEAD_DIM)
            .transpose(1, 0, 2, 3)
            .reshape(kv_local, STRETCH * group_size, HEAD_DIM)
        )
        row_of = row_start + jnp.arange(STRETCH * group_size, dtype=jnp.int32) // group_size
        new_keys = (
            key_upd.reshape(rows_all, kv_local, HEAD_DIM).transpose(1, 0, 2).astype(jnp.float32)
        )
        new_vals = value_upd.reshape(rows_all, kv_local, HEAD_DIM).transpose(1, 0, 2)
        new_scores = (
            jnp.einsum("kqd,kjd->kqj", query_rows, new_keys, precision=full_prec) * score_scale
        )
        new_ok = jnp.arange(rows_all, dtype=jnp.int32)[None, :] <= row_of[:, None]
        new_scores = jnp.where(new_ok[None], new_scores, masked_score)

        def kept_scores(blk_idx):
            blk_start = blk_idx * key_block
            key_tile = (
                lax.dynamic_slice_in_dim(kv_store[0], blk_start, key_block, 0)
                .reshape(key_block, kv_local, HEAD_DIM)
                .transpose(1, 0, 2)
                .astype(jnp.float32)
            )
            scores = (
                jnp.einsum("kqd,kjd->kqj", query_rows, key_tile, precision=full_prec) * score_scale
            )
            key_ok = blk_start + jnp.arange(key_block, dtype=jnp.int32) < prefix
            return jnp.where(key_ok[None, None, :], scores, masked_score)

        row_max = jnp.max(new_scores, axis=-1)
        row_sum = jnp.sum(jnp.exp(new_scores - row_max[..., None]), axis=-1)

        def stat_step(blk_idx, carry):
            run_max, run_sum = carry
            scores = kept_scores(blk_idx)
            next_max = jnp.maximum(run_max, jnp.max(scores, axis=-1))
            next_sum = run_sum * jnp.exp(run_max - next_max) + jnp.sum(
                jnp.exp(scores - next_max[..., None]), axis=-1
            )
            return (next_max, next_sum)

        row_max, row_sum = lax.fori_loop(0, block_total, stat_step, (row_max, row_sum))
        new_probs = (jnp.exp(new_scores - row_max[..., None]) / row_sum[..., None]).astype(
            jnp.bfloat16
        )
        weighted = jnp.einsum(
            "kqj,kjd->kqd", new_probs, new_vals, preferred_element_type=jnp.float32
        )

        def value_step(blk_idx, total):
            scores = kept_scores(blk_idx)
            probs = (jnp.exp(scores - row_max[..., None]) / row_sum[..., None]).astype(jnp.bfloat16)
            value_tile = (
                lax.dynamic_slice_in_dim(kv_store[1], blk_idx * key_block, key_block, 0)
                .reshape(key_block, kv_local, HEAD_DIM)
                .transpose(1, 0, 2)
            )
            return total + jnp.einsum(
                "kqj,kjd->kqd", probs, value_tile, preferred_element_type=jnp.float32
            )

        weighted = lax.fori_loop(0, block_total, value_step, weighted)
        mixed_heads = (
            weighted.reshape(kv_local, STRETCH, group_size, HEAD_DIM)
            .transpose(1, 0, 2, 3)
            .reshape(STRETCH, local_cols)
            .astype(jnp.bfloat16)
        )
        partials = jnp.dot(mixed_heads, out_w, preferred_element_type=jnp.float32)
        attn_part = lax.psum_scatter(
            partials.astype(jnp.bfloat16), "tensor", scatter_dimension=1, tiled=True
        ).astype(jnp.float32)
        hid_part = (x_part.astype(jnp.float32) + attn_part).astype(jnp.bfloat16)
        live_now = valid & (slot_num < live_count)
        attn_vals = jnp.where(live_now, attn_part.astype(jnp.bfloat16), jnp.zeros_like(hid_part))
        hid_vals = jnp.where(live_now, hid_part, jnp.zeros_like(hid_part))
        attn_buf = jnp.where(
            valid, lax.dynamic_update_slice(attn_buf, attn_vals, (row_start, 0)), attn_buf
        )
        hid_buf = jnp.where(
            valid, lax.dynamic_update_slice(hid_buf, hid_vals, (row_start, 0)), hid_buf
        )
        if tick_num + 1 < tick_total:
            joined = lax.all_gather(hid_part, "tensor", axis=1, tiled=True)
            incoming = from_behind(joined, "section", 1)
    return (attn_buf[None], hid_buf[None])


def solution(mesh):
    return jax.shard_map(
        shards,
        mesh=mesh,
        in_specs=(
            P("dp", "tensor"),
            P("section", "dp", None, None, "tensor"),
            P("section", None),
            P("section", "dp", "tensor"),
            P("section", "dp", None, "tensor"),
            P("section", "tensor", "dp"),
            P("dp"),
            P("dp"),
        ),
        out_specs=(P("section", "dp", "tensor"), P("section", "dp", "tensor")),
        check_vma=False,
    )
```

profile of v0, /device:TPU:7, one launch (start us, length us, event | category | flops | bytes accessed | tf_op | source)
XLA Modules:
  0.0 1117.0 jit_solution(12745088687760437559)
XLA Ops:
  12.9 35.9 %all-gather.9.cloned.1.call-done = bf16[256,5120]{1,0:T(8,128)(2,1)} async-done(((bf16[256,2560]{1,0:T(8,128)(2,1)}), bf16[256,5120]{1,0:T(8,128)(2,1)}) %all-gather.9.cloned.1.call-update) | async-done | bytes 2621456 | tf_op jit(solution)/shard_map/all_gather | solution.py:72
  50.7 98.9 %all-gather.13.cloned.1.call-done = bf16[1,5120,2,256]{3,2,0,1:T(2,128)(2,1)} async-done(((bf16[1,1280,2,256]{3,2,0,1:T(2,128)(2,1)}), bf16[1,5120,2,256]{3,2,0,1:T(2,128)(2,1)}) %all-gather.13.cloned.1.call-update) | async-done | bytes 5242896 | tf_op jit(solution)/shard_map/all_gather | solution.py:44
  149.6 3.4 copy.299
  156.2 220.2 %all-gather.11.cloned.1.call-done = bf16[1,5120,1280]{2,1,0:T(8,128)(2,1)} async-done(((bf16[1,1280,1280]{2,1,0:T(8,128)(2,1)}), bf16[1,5120,1280]{2,1,0:T(8,128)(2,1)}) %all-gather.11.cloned.1.call-update) | async-done | bytes 13107216 | tf_op jit(solution)/shard_map/all_gather | solution.py:43
  376.4 18.3 %copy.211 = bf16[1280,5120]{1,0:T(8,128)(2,1)} copy(bf16[1280,5120]{0,1:T(8,128)(2,1)} %bitcast.419) | data formatting | bytes 26214400 | tf_op jit(solution)/shard_map/dot_general | solution.py:89
  394.8 6.7 fusion.83
  404.7 6.1 while.140
  413.4 13.5 %while.141 = (s32[]{:T(128)}, f32[2,640,128]{2,1,0:T(8,128)}, s32[]{:T(128)}, bf16[2,1024,256]{1,2,0:T(8,128)(2,1)S(1)}, f32[2,640,128]{2,1,0:T(8,128)S(1)}, /*i...) while((s32[]{:T(128)}, f32[2,640,128]{2,1,0:T(8,128)}, ...), condition=%wide.region_8.9_spmd, body=%wide.region_7.8_spmd.sunk | while | flops 1177846784 | bytes 9317551 | solution.py:166
  429.0 173.8 %all-gather.15.cloned.1.call-done = bf16[1,1280,5120]{2,1,0:T(8,128)(2,1)} async-done(((bf16[1,1280,1280]{2,1,0:T(8,128)(2,1)}), bf16[1,1280,5120]{2,1,0:T(8,128)(2,1)}) %all-gather.15.cloned.1.call-update) | async-done | bytes 13107216 | tf_op jit(solution)/shard_map/all_gather | solution.py:46
  602.9 7.7 fusion.40
  611.4 19.6 %reduce-scatter.6.cloned.1.call-done = bf16[128,2560]{1,0:T(8,128)(2,1)} async-done(((bf16[128,5120]{1,0:T(8,128)(2,1)}), bf16[128,2560]{1,0:T(8,128)(2,1)}) %reduce-scatter.6.cloned.1.call-update) | async-done | bytes 655376 | tf_op jit(solution)/shard_map/reduce_scatter | solution.py:174
  633.7 24.4 %all-gather.17.cloned.1.call-done = bf16[128,5120]{1,0:T(8,128)(2,1)} async-done(((bf16[128,2560]{1,0:T(8,128)(2,1)}), bf16[128,5120]{1,0:T(8,128)(2,1)}) %all-gather.17.cloned.1.call-update) | async-done | bytes 1310736 | tf_op jit(solution)/shard_map/all_gather | solution.py:188
  665.3 3.8 fusion.103
  669.2 6.8 fusion.81
  680.0 6.1 while.142
  686.1 2.6 fusion.90
  688.8 13.2 %while.143 = (s32[]{:T(128)}, f32[2,640,128]{2,1,0:T(8,128)}, s32[]{:T(128)}, bf16[2,1024,256]{1,2,0:T(8,128)(2,1)S(1)}, f32[2,640,128]{2,1,0:T(8,128)S(1)}, /*i...) while((s32[]{:T(128)}, f32[2,640,128]{2,1,0:T(8,128)}, ...), condition=%wide.region_18.19_spmd, body=%wide.region_17.18_spmd.sunk | while | flops 1177846784 | bytes 9317551 | solution.py:166
  704.1 7.7 fusion.43
  713.0 35.9 %reduce-scatter.8.cloned.1.call-done = bf16[128,2560]{1,0:T(8,128)(2,1)} async-done(((bf16[128,5120]{1,0:T(8,128)(2,1)}), bf16[128,2560]{1,0:T(8,128)(2,1)}) %reduce-scatter.8.cloned.1.call-update) | async-done | bytes 655376 | tf_op jit(solution)/shard_map/reduce_scatter | solution.py:174
  749.0 3.3 select_dynamic-update-slice_fusion.2
  752.4 24.4 %all-gather.19.cloned.1.call-done = bf16[128,5120]{1,0:T(8,128)(2,1)} async-done(((bf16[128,2560]{1,0:T(8,128)(2,1)}), bf16[128,5120]{1,0:T(8,128)(2,1)}) %all-gather.19.cloned.1.call-update) | async-done | bytes 1310736 | tf_op jit(solution)/shard_map/all_gather | solution.py:188
  778.5 3.7 collective-permute-done.1
  784.6 3.8 fusion.100
  788.5 6.9 fusion.79
  799.5 6.1 while.144
  808.3 13.1 %while.145 = (s32[]{:T(128)}, f32[2,640,128]{2,1,0:T(8,128)}, s32[]{:T(128)}, bf16[2,1024,256]{1,2,0:T(8,128)(2,1)S(1)}, f32[2,640,128]{2,1,0:T(8,128)S(1)}, /*i...) while((s32[]{:T(128)}, f32[2,640,128]{2,1,0:T(8,128)}, ...), condition=%wide.region_28.29_spmd, body=%wide.region_27.28_spmd.sunk | while | flops 1177846784 | bytes 9317551 | solution.py:166
  823.6 7.7 fusion.46
  831.8 36.7 %reduce-scatter.10.cloned.1.call-done = bf16[128,2560]{1,0:T(8,128)(2,1)} async-done(((bf16[128,5120]{1,0:T(8,128)(2,1)}), bf16[128,2560]{1,0:T(8,128)(2,1)}) %reduce-scatter.10.cloned.1.call-update) | async-done | bytes 655376 | tf_op jit(solution)/shard_map/reduce_scatter | solution.py:174
  868.5 3.3 select_dynamic-update-slice_fusion.1
  871.9 24.4 %all-gather.21.cloned.1.call-done = bf16[128,5120]{1,0:T(8,128)(2,1)} async-done(((bf16[128,2560]{1,0:T(8,128)(2,1)}), bf16[128,5120]{1,0:T(8,128)(2,1)}) %all-gather.21.cloned.1.call-update) | async-done | bytes 1310736 | tf_op jit(solution)/shard_map/all_gather | solution.py:188
  898.6 3.1 collective-permute-done.2
  904.1 3.8 fusion.97
  908.0 6.8 fusion.77
  918.8 6.1 while.146
  925.0 2.6 fusion.92
  927.6 13.1 %while.147 = (s32[]{:T(128)}, f32[2,640,128]{2,1,0:T(8,128)}, s32[]{:T(128)}, bf16[2,1024,256]{1,2,0:T(8,128)(2,1)S(1)}, f32[2,640,128]{2,1,0:T(8,128)S(1)}, /*i...) while((s32[]{:T(128)}, f32[2,640,128]{2,1,0:T(8,128)}, ...), condition=%wide.region_38.39_spmd, body=%wide.region_37.38_spmd.sunk | while | flops 1177846784 | bytes 9317551 | solution.py:166
  942.9 7.7 fusion.49
  950.9 36.9 %reduce-scatter.12.cloned.1.call-done = bf16[128,2560]{1,0:T(8,128)(2,1)} async-done(((bf16[128,5120]{1,0:T(8,128)(2,1)}), bf16[128,2560]{1,0:T(8,128)(2,1)}) %reduce-scatter.12.cloned.1.call-update) | async-done | bytes 655376 | tf_op jit(solution)/shard_map/reduce_scatter | solution.py:174
  987.8 3.4 select_dynamic-update-slice_fusion
  991.3 24.4 %all-gather.23.cloned.1.call-done = bf16[128,5120]{1,0:T(8,128)(2,1)} async-done(((bf16[128,2560]{1,0:T(8,128)(2,1)}), bf16[128,5120]{1,0:T(8,128)(2,1)}) %all-gather.23.cloned.1.call-update) | async-done | bytes 1310736 | tf_op jit(solution)/shard_map/all_gather | solution.py:188
  1017.3 3.7 collective-permute-done.3
  1023.4 3.8 fusion.94
  1027.3 6.8 fusion.75
  1038.0 6.1 while.148
  1046.8 13.1 %while.149 = (s32[]{:T(128)}, f32[2,640,128]{2,1,0:T(8,128)}, s32[]{:T(128)}, bf16[2,1024,256]{1,2,0:T(8,128)(2,1)S(1)}, f32[2,640,128]{2,1,0:T(8,128)S(1)}, /*i...) while((s32[]{:T(128)}, f32[2,640,128]{2,1,0:T(8,128)}, ...), condition=%wide.region_48.49_spmd, body=%wide.region_47.48_spmd.sunk | while | flops 1177846784 | bytes 9317551 | solution.py:166
  1062.3 7.7 fusion.52
  1073.6 33.5 %reduce-scatter.14.cloned.1.call-done = bf16[128,2560]{1,0:T(8,128)(2,1)} async-done(((bf16[128,5120]{1,0:T(8,128)(2,1)}), bf16[128,2560]{1,0:T(8,128)(2,1)}) %reduce-scatter.14.cloned.1.call-update) | async-done | bytes 655376 | tf_op jit(solution)/shard_map/reduce_scatter | solution.py:174
  1107.1 3.1 fusion.88
  (476 shorter events, 170.7 us)
Async XLA Ops:
  7.2 41.7 %all-gather.9.cloned.1.call-start = ((), (), s32[]{:S(2)}) async-start(), calls=%async_computation.5 | async-start | bytes 3932160 | tf_op jit(solution)/shard_map/all_gather | solution.py:72
  7.9 141.7 %all-gather.13.cloned.1.call-start = ((), (), s32[]{:S(2)}) async-start(), calls=%async_computation.7 | async-start | bytes 6553600 | tf_op jit(solution)/shard_map/all_gather | solution.py:44
  8.6 367.8 %all-gather.11.cloned.1.call-start = ((), (), s32[]{:S(2)}) async-start(), calls=%async_computation.6 | async-start | bytes 16384000 | tf_op jit(solution)/shard_map/all_gather | solution.py:43
  9.4 593.5 %all-gather.15.cloned.1.call-start = ((), (), s32[]{:S(2)}) async-start(), calls=%async_computation.8 | async-start | bytes 16384000 | tf_op jit(solution)/shard_map/all_gather | solution.py:46
  10.0 621.0 %reduce-scatter.6.cloned.1.call-start = ((), (), s32[]{:S(2)}) async-start(), calls=%async_computation.9 | async-start | bytes 1966080 | tf_op jit(solution)/shard_map/reduce_scatter | solution.py:174
  50.7 344.1 %copy-start.8 = (bf16[128,5120]{1,0:T(8,128)(2,1)}, bf16[128,5120]{1,0:T(8,128)(2,1)S(1)}, u32[]{:S(2)}) copy-start(bf16[128,5120]{1,0:T(8,128)(2,1)S(1)} %get-tuple-element.1529) | copy-start | bytes 3932164
  156.2 254.6 %copy-start.50 = (bf16[256,256]{0,1:T(8,128)(2,1)}, bf16[256,256]{0,1:T(8,128)(2,1)S(1)}, u32[]{:S(2)}) copy-start(bf16[256,256]{0,1:T(8,128)(2,1)S(1)} %constant_dynamic-update-slice_fusion.8) | copy-start | bytes 393220
  156.2 246.3 %copy-start.21 = (bf16[256,256]{0,1:T(8,128)(2,1)}, bf16[256,256]{0,1:T(8,128)(2,1)S(1)}, u32[]{:S(2)}) copy-start(bf16[256,256]{0,1:T(8,128)(2,1)S(1)} %constant_dynamic-update-slice_fusion.9) | copy-start | bytes 393220
  610.6 47.5 %all-gather.17.cloned.1.call-start = ((), (), s32[]{:S(2)}) async-start(), calls=%async_computation.10 | async-start | bytes 1966080 | tf_op jit(solution)/shard_map/all_gather | solution.py:188
  632.3 27.1 %copy-start.65 = (f32[128,64]{0,1:T(8,128)S(1)}, f32[128,64]{0,1:T(8,128)}, u32[]{:S(2)}) copy-start(f32[128,64]{0,1:T(8,128)} %get-tuple-element.1595) | copy-start | bytes 98308
  632.3 27.2 %copy-start.66 = (f32[128,64]{0,1:T(8,128)S(1)}, f32[128,64]{0,1:T(8,128)}, u32[]{:S(2)}) copy-start(f32[128,64]{0,1:T(8,128)} %get-tuple-element.1596) | copy-start | bytes 98308
  632.3 28.0 %copy-start.22 = (bf16[256,256]{0,1:T(8,128)(2,1)S(1)}, bf16[256,256]{0,1:T(8,128)(2,1)}, u32[]{:S(2)}) copy-start(bf16[256,256]{0,1:T(8,128)(2,1)} %copy-done.21) | copy-start | bytes 393220
  632.3 28.0 %copy-start.51 = (bf16[256,256]{0,1:T(8,128)(2,1)S(1)}, bf16[256,256]{0,1:T(8,128)(2,1)}, u32[]{:S(2)}) copy-start(bf16[256,256]{0,1:T(8,128)(2,1)} %copy-done.50) | copy-start | bytes 393220
  633.7 115.3 %reduce-scatter.8.cloned.1.call-start = ((), (), s32[]{:S(2)}) async-start(), calls=%async_computation.11 | async-start | bytes 1966080 | tf_op jit(solution)/shard_map/reduce_scatter | solution.py:174
  658.1 5.3 collective-permute-start
  711.8 65.0 %all-gather.19.cloned.1.call-start = ((), (), s32[]{:S(2)}) async-start(), calls=%async_computation.12 | async-start | bytes 1966080 | tf_op jit(solution)/shard_map/all_gather | solution.py:188
  749.0 29.1 %copy-start.63 = (f32[128,64]{0,1:T(8,128)S(1)}, f32[128,64]{0,1:T(8,128)}, u32[]{:S(2)}) copy-start(f32[128,64]{0,1:T(8,128)} %get-tuple-element.1597) | copy-start | bytes 98308
  749.0 29.2 %copy-start.64 = (f32[128,64]{0,1:T(8,128)S(1)}, f32[128,64]{0,1:T(8,128)}, u32[]{:S(2)}) copy-start(f32[128,64]{0,1:T(8,128)} %get-tuple-element.1598) | copy-start | bytes 98308
  749.0 29.3 %copy-start.67 = (s32[640]{0:T(1024)S(1)}, s32[640]{0:T(1024)}, u32[]{:S(2)}) copy-start(s32[640]{0:T(1024)} %get-tuple-element.1615) | copy-start | bytes 7684
  749.0 29.4 %copy-start.26 = (bf16[256,256]{0,1:T(8,128)(2,1)S(1)}, bf16[256,256]{0,1:T(8,128)(2,1)}, u32[]{:S(2)}) copy-start(bf16[256,256]{0,1:T(8,128)(2,1)} %copy-done.25) | copy-start | bytes 393220
  749.0 29.4 %copy-start.53 = (bf16[256,256]{0,1:T(8,128)(2,1)S(1)}, bf16[256,256]{0,1:T(8,128)(2,1)}, u32[]{:S(2)}) copy-start(bf16[256,256]{0,1:T(8,128)(2,1)} %copy-done.52) | copy-start | bytes 393220
  752.3 32.2 %copy-start = (bf16[256,2560]{1,0:T(8,128)(2,1)}, bf16[256,2560]{1,0:T(8,128)(2,1)S(1)}, u32[]{:S(2)}) copy-start(bf16[256,2560]{1,0:T(8,128)(2,1)S(1)} %get-tuple-element.1574) | copy-start | bytes 3932164
  752.3 26.1 %copy-start.24 = (bf16[256,256]{0,1:T(8,128)(2,1)S(1)}, bf16[256,256]{0,1:T(8,128)(2,1)}, u32[]{:S(2)}) copy-start(bf16[256,256]{0,1:T(8,128)(2,1)} %copy-done.23) | copy-start | bytes 393220
  752.3 26.1 %copy-start.28 = (bf16[256,256]{0,1:T(8,128)(2,1)S(1)}, bf16[256,256]{0,1:T(8,128)(2,1)}, u32[]{:S(2)}) copy-start(bf16[256,256]{0,1:T(8,128)(2,1)} %copy-done.27) | copy-start | bytes 393220
  752.4 116.1 %reduce-scatter.10.cloned.1.call-start = ((), (), s32[]{:S(2)}) async-start(), calls=%async_computation.13 | async-start | bytes 1966080 | tf_op jit(solution)/shard_map/reduce_scatter | solution.py:174
  776.8 5.4 collective-permute-start.1
  831.3 37.2 %copy-start.1 = (bf16[256,2560]{1,0:T(8,128)(2,1)S(1)}, bf16[256,2560]{1,0:T(8,128)(2,1)}, u32[]{:S(2)}) copy-start(bf16[256,2560]{1,0:T(8,128)(2,1)} %copy-done) | copy-start | bytes 3932164
  831.3 65.0 %all-gather.21.cloned.1.call-start = ((), (), s32[]{:S(2)}) async-start(), calls=%async_computation.14 | async-start | bytes 1966080 | tf_op jit(solution)/shard_map/all_gather | solution.py:188
  868.5 29.1 %copy-start.61 = (f32[128,64]{0,1:T(8,128)S(1)}, f32[128,64]{0,1:T(8,128)}, u32[]{:S(2)}) copy-start(f32[128,64]{0,1:T(8,128)} %get-tuple-element.1599) | copy-start | bytes 98308
  868.5 29.2 %copy-start.62 = (f32[128,64]{0,1:T(8,128)S(1)}, f32[128,64]{0,1:T(8,128)}, u32[]{:S(2)}) copy-start(f32[128,64]{0,1:T(8,128)} %get-tuple-element.1600) | copy-start | bytes 98308
  868.5 30.0 %copy-start.40 = (bf16[256,256]{0,1:T(8,128)(2,1)S(1)}, bf16[256,256]{0,1:T(8,128)(2,1)}, u32[]{:S(2)}) copy-start(bf16[256,256]{0,1:T(8,128)(2,1)} %copy-done.39) | copy-start | bytes 393220
  868.5 30.0 %copy-start.42 = (bf16[256,256]{0,1:T(8,128)(2,1)S(1)}, bf16[256,256]{0,1:T(8,128)(2,1)}, u32[]{:S(2)}) copy-start(bf16[256,256]{0,1:T(8,128)(2,1)} %copy-done.41) | copy-start | bytes 393220
  871.8 32.1 %copy-start.2 = (bf16[256,2560]{1,0:T(8,128)(2,1)}, bf16[256,2560]{1,0:T(8,128)(2,1)S(1)}, u32[]{:S(2)}) copy-start(bf16[256,2560]{1,0:T(8,128)(2,1)S(1)} %get-tuple-element.1573) | copy-start | bytes 3932164
  871.8 26.7 %copy-start.30 = (bf16[256,256]{0,1:T(8,128)(2,1)S(1)}, bf16[256,256]{0,1:T(8,128)(2,1)}, u32[]{:S(2)}) copy-start(bf16[256,256]{0,1:T(8,128)(2,1)} %copy-done.29) | copy-start | bytes 393220
  871.9 26.7 %copy-start.32 = (bf16[256,256]{0,1:T(8,128)(2,1)S(1)}, bf16[256,256]{0,1:T(8,128)(2,1)}, u32[]{:S(2)}) copy-start(bf16[256,256]{0,1:T(8,128)(2,1)} %copy-done.31) | copy-start | bytes 393220
  871.9 115.9 %reduce-scatter.12.cloned.1.call-start = ((), (), s32[]{:S(2)}) async-start(), calls=%async_computation.15 | async-start | bytes 1966080 | tf_op jit(solution)/shard_map/reduce_scatter | solution.py:174
  896.3 5.4 collective-permute-start.2
  950.6 37.2 %copy-start.3 = (bf16[256,2560]{1,0:T(8,128)(2,1)S(1)}, bf16[256,2560]{1,0:T(8,128)(2,1)}, u32[]{:S(2)}) copy-start(bf16[256,2560]{1,0:T(8,128)(2,1)} %copy-done.2) | copy-start | bytes 3932164
  950.6 65.0 %all-gather.23.cloned.1.call-start = ((), (), s32[]{:S(2)}) async-start(), calls=%async_computation.16 | async-start | bytes 1966080 | tf_op jit(solution)/shard_map/all_gather | solution.py:188
  987.8 29.1 %copy-start.60 = (f32[128,64]{0,1:T(8,128)S(1)}, f32[128,64]{0,1:T(8,128)}, u32[]{:S(2)}) copy-start(f32[128,64]{0,1:T(8,128)} %get-tuple-element.1586) | copy-start | bytes 98308
  987.8 29.2 %copy-start.59 = (f32[128,64]{0,1:T(8,128)S(1)}, f32[128,64]{0,1:T(8,128)}, u32[]{:S(2)}) copy-start(f32[128,64]{0,1:T(8,128)} %get-tuple-element.1585) | copy-start | bytes 98308
  987.8 29.3 %copy-start.68 = (s32[640]{0:T(1024)S(1)}, s32[640]{0:T(1024)}, u32[]{:S(2)}) copy-start(s32[640]{0:T(1024)} %get-tuple-element.1613) | copy-start | bytes 7684
  987.8 29.5 %copy-start.45 = (bf16[256,256]{0,1:T(8,128)(2,1)S(1)}, bf16[256,256]{0,1:T(8,128)(2,1)}, u32[]{:S(2)}) copy-start(bf16[256,256]{0,1:T(8,128)(2,1)} %copy-done.44) | copy-start | bytes 393220
  987.8 29.5 %copy-start.47 = (bf16[256,256]{0,1:T(8,128)(2,1)S(1)}, bf16[256,256]{0,1:T(8,128)(2,1)}, u32[]{:S(2)}) copy-start(bf16[256,256]{0,1:T(8,128)(2,1)} %copy-done.46) | copy-start | bytes 393220
  991.2 32.2 %copy-start.4 = (bf16[256,2560]{1,0:T(8,128)(2,1)}, bf16[256,2560]{1,0:T(8,128)(2,1)S(1)}, u32[]{:S(2)}) copy-start(bf16[256,2560]{1,0:T(8,128)(2,1)S(1)} %get-tuple-element.1572) | copy-start | bytes 3932164
  991.2 115.9 %reduce-scatter.14.cloned.1.call-start = ((), (), s32[]{:S(2)}) async-start(), calls=%async_computation.17 | async-start | bytes 1966080 | tf_op jit(solution)/shard_map/reduce_scatter | solution.py:174
  1015.6 5.4 collective-permute-start.3
  1072.6 34.6 %copy-start.7 = (bf16[128,5120]{1,0:T(8,128)(2,1)S(1)}, bf16[128,5120]{1,0:T(8,128)(2,1)}, u32[]{:S(2)}) copy-start(bf16[128,5120]{1,0:T(8,128)(2,1)} %copy-done.6) | copy-start | bytes 3932164
  (38 other events, 183.0 us)
Sparse Core Ops, SparseCore 0:
  9.5 39.2 all-gather.8
  50.4 99.1 all-gather.12
  151.2 225.2 all-gather.10
  377.9 224.9 all-gather.14
  610.7 20.2 reduce-scatter.5
  633.8 24.2 all-gather.16
  711.9 37.0 reduce-scatter.7
  752.5 24.2 all-gather.18
  831.5 36.9 reduce-scatter.9
  872.0 24.2 all-gather.20
  950.8 36.9 reduce-scatter.11
  991.3 24.2 all-gather.22
  1070.1 36.9 reduce-scatter.13
where the time goes:
time: 1130 us; the launch traced here: 1120 us
  waiting for transfers between devices  805 us (71%)
  matrix products  170 us (15%)
  other arithmetic  62.4 us (6%)
  local copies, waits for them, and re-layouts  54.7 us (5%)
  between operations  17.4 us (2%)
    all_gather x1, waiting for transfers between devices, shards(): lax.all_gather(w_query, 'dp', axis=1, tiled=True)  220 us
    all_gather x1, waiting for transfers between devices, shards(): out_w = lax.all_gather(w_out, 'dp', axis=2, tiled=True)[0]  174 us
    reduce_scatter x5, waiting for transfers between devices, shards(): lax.psum_scatter(partials.astype(jnp.bfloat16), 'tensor', scatter_dimensi...  163 us
    all_gather x1, waiting for transfers between devices, shards(): lax.all_gather(w_keyval, 'dp', axis=1, tiled=True)  98.9 us
    all_gather x4, waiting for transfers between devices, shards(): joined = lax.all_gather(hid_part, 'tensor', axis=1, tiled=True)  97.5 us
    dot_general x5, matrix products, shards(): partials = jnp.dot(mixed_heads, out_w, preferred_element_type=jnp.float32)  38.5 us
    dot_general x20, matrix products, kept_scores(): jnp.einsum('kqd,kjd->kqj', query_rows, key_tile, precision=full_prec)  38.3 us
    all_gather x1, waiting for transfers between devices, shards(): inputs_all = lax.all_gather(hidden_in, 'tensor', axis=1, tiled=True)  35.9 us
  transfers between devices with their start and end apart: 17, of which 17 were waited for; matrix products, arithmetic and copies ran while one was open for 6% of the time, Pallas kernels for 0%

commit v1 on v0

--- a/solution.py
+++ b/solution.py
@@ -1,6 +1,10 @@
+import functools
+
 import jax
 import jax.numpy as jnp
 from jax import lax
+from jax.experimental import pallas as pl
+from jax.experimental.pallas import tpu as pltpu
 from jax.sharding import PartitionSpec as P
 
 HEAD_DIM = 128
@@ -190,9 +194,400 @@
     return (attn_buf[None], hid_buf[None])
 
 
+def relay_kernel(
+    slots, sections, groups, tensors,
+    x_in, wqkv_q, wqkv_kv, w_out, gain, kv, cos_ref, sin_ref, bias_ref,
+    attn_ref, hid_ref,
+    xbuf, q_send, q_recv, ss_send, ss_recv, q_own, q_cat, k_all, v_all,
+    heads, p_send, p_recv, x_next, a_send, a_recv, h_recv, h_send,
+    xin_s, x_r, q_s, q_r, ss_s, ss_r, h_s, h_r, p_s, p_r, xn_s, a_s, a_r, hc_s, hc_r, loc,
+):
+    s = lax.axis_index("section")
+    g = lax.axis_index("dp")
+    t = lax.axis_index("tensor")
+    last = sections - 1
+    per_t = groups // tensors
+    width = x_next.shape[-1]
+    q_cols = wqkv_q.shape[1]
+    kv_cols = kv.shape[2]
+    kv_heads = kv_cols // HEAD_DIM
+    head_total = q_cols // HEAD_DIM
+    group_size = head_total // kv_heads
+    kept = kv.shape[1]
+    half_cols = group_size * HEAD_DIM
+
+    def dev(sec, grp, ten):
+        return {"section": sec, "dp": grp, "tensor": ten}
+
+    def remote(src, dst, send, recv, target):
+        return pltpu.make_async_remote_copy(
+            src_ref=src, dst_ref=dst, send_sem=send, recv_sem=recv,
+            device_id=target, device_id_type=pl.DeviceIdType.MESH,
+        )
+
+    barrier = pltpu.get_barrier_semaphore()
+    for dg in range(groups):
+        for dt in range(tensors):
+            if dg or dt:
+                pl.semaphore_signal(
+                    barrier, inc=1,
+                    device_id=dev(s, lax.rem(g + dg, groups), lax.rem(t + dt, tensors)),
+                    device_id_type=pl.DeviceIdType.MESH,
+                )
+
+    @pl.when(s > 0)
+    def _():
+        pl.semaphore_signal(
+            barrier, inc=1, device_id=dev(s - 1, g, t), device_id_type=pl.DeviceIdType.MESH
+        )
+
+    @pl.when(s < last)
+    def _():
+        pl.semaphore_signal(
+            barrier, inc=1, device_id=dev(s + 1, g, t), device_id_type=pl.DeviceIdType.MESH
+        )
+
+    edge = jnp.where(s > 0, 1, 0) + jnp.where(s < last, 1, 0)
+    pl.semaphore_wait(barrier, groups * tensors - 1 + edge)
+
+    def input_copy(j, c, td):
+        return remote(
+            x_in.at[pl.ds(j * STRETCH, STRETCH), pl.ds(c * width, width)],
+            xbuf.at[j, g], xin_s.at[j, c, td], x_r.at[j, g], dev(0, per_t * t + c, td),
+        )
+
+    def local_copy(j, c):
+        return pltpu.make_async_copy(
+            x_in.at[pl.ds(j * STRETCH, STRETCH), pl.ds(c * width, width)], xbuf.at[j, g], loc.at[j]
+        )
+
+    def for_inputs(do):
+        for j in range(slots):
+            for c in range(per_t):
+                for td in range(tensors):
+                    own = (per_t * t + c == g) & (td == t)
+
+                    @pl.when((s == 0) & jnp.logical_not(own))
+                    def _():
+                        do(input_copy(j, c, td))
+
+    for_inputs(lambda copy: copy.start())
+    is_local = (s == 0) & (g // per_t == t)
+    for j in range(slots):
+        for c in range(per_t):
+
+            @pl.when((s == 0) & (per_t * t + c == g))
+            def _():
+                local_copy(j, c).start()
+
+    for h in range(kv_heads):
+        piece = kv[0, :, h * HEAD_DIM : (h + 1) * HEAD_DIM]
+        k_all[h, :kept, :HEAD_DIM] = piece
+        k_all[h, :kept, HEAD_DIM:] = piece
+        v_all[h, :kept, :] = kv[1, :, h * HEAD_DIM : (h + 1) * HEAD_DIM]
+        fresh = k_all.shape[1] - kept
+        k_all[h, kept:, :] = jnp.zeros((fresh, 2 * HEAD_DIM), jnp.bfloat16)
+        v_all[h, kept:, :] = jnp.zeros((fresh, HEAD_DIM), jnp.bfloat16)
+    for j in range(slots):
+        for c in range(per_t):
+
+            @pl.when((s == 0) & (per_t * t + c == g))
+            def _():
+                local_copy(j, c).wait()
+
+    def q_copy(j, src, dst_slot, sem, target):
+        return remote(q_send.at[j, src], q_recv.at[j, dst_slot], q_s.at[j, src], q_r.at[j, sem], target)
+
+    def ss_copy(j, src, dst_slot, sem, target):
+        return remote(
+            ss_send.at[j, src], ss_recv.at[j, dst_slot], ss_s.at[j, src], ss_r.at[j, sem], target
+        )
+
+    def h_copy(j, part, slot, peer):
+        cols = pl.ds(part * half_cols, half_cols)
+        return remote(
+            heads.at[j, slot, :, cols], heads.at[j, slot, :, cols],
+            h_s.at[j, peer, part], h_r.at[j, slot, part], dev(s, peer, t),
+        )
+
+    def p_copy(j, tr):
+        return remote(
+            p_send.at[j, tr], p_recv.at[j, tr], p_s.at[j, tr], p_r.at[j, tr],
+            dev(s, g, lax.rem(t + 1, tensors)),
+        )
+
+    def x_copy(j, tr, sec):
+        return remote(x_next.at[j, tr], xbuf.at[j, tr], xn_s.at[j, tr], x_r.at[j, tr], dev(sec, g, t))
+
+    def a_copy(j, tr, c, peer):
+        return remote(a_send.at[j, tr], a_recv.at[j, c], a_s.at[j, tr], a_r.at[j, c], dev(s, peer, t))
+
+    def hc_copy(j, sec):
+        return remote(h_send.at[j], h_recv.at[j], hc_s.at[j], hc_r.at[j], dev(sec, g, t))
+
+    def rotate(values, cosine, sine):
+        return values * cosine + pltpu.roll(values, HEAD_DIM // 2, 1) * sine
+
+    @pl.loop(0, slots)
+    def _(j):
+        row = pl.multiple_of(j * STRETCH, STRETCH)
+        for k in (2, 1, 3, 0) if groups == 4 else list(range(1, groups)) + [0]:
+            d = lax.rem(g + k, groups)
+            arrives = jnp.logical_not(is_local) | (d != g)
+
+            @pl.when(arrives)
+            def _():
+                x_copy(j, d, s).wait_recv()
+
+            x_val = xbuf[j, d].astype(jnp.float32)
+            square = jnp.sum(x_val * x_val, axis=1, keepdims=True)
+            ss_send[j, d] = jnp.broadcast_to(square, (STRETCH, HEAD_DIM))
+            x_gain = (x_val * gain[...]).astype(jnp.bfloat16)
+            part_q = jnp.dot(x_gain, wqkv_q[...], preferred_element_type=jnp.float32)
+            part_kv = jnp.dot(x_gain, wqkv_kv[...], preferred_element_type=jnp.float32)
+            if k:
+                q_send[j, d, :, :q_cols] = part_q.astype(jnp.bfloat16)
+                q_send[j, d, :, q_cols:] = part_kv.astype(jnp.bfloat16)
+                ss_copy(j, d, g, g, dev(s, d, t)).start()
+                q_copy(j, d, g, g, dev(s, d, t)).start()
+            else:
+                q_own[:, :q_cols] = part_q
+                q_own[:, q_cols:] = part_kv
+        square = ss_send[j, g]
+        for k in range(1, groups):
+            src = lax.rem(g + k, groups)
+            ss_copy(j, src, src, src, dev(s, src, t)).wait_recv()
+            q_copy(j, src, src, src, dev(s, src, t)).wait_recv()
+            square = square + ss_recv[j, src]
+        scale = lax.rsqrt(square * (1.0 / (groups * width)) + eps_norm)
+        cosine = cos_ref[pl.ds(row, STRETCH), :]
+        sine = sin_ref[pl.ds(row, STRETCH), :]
+
+        def total(col):
+            value = q_own[:, col : col + HEAD_DIM]
+            for k in range(1, groups):
+                src = lax.rem(g + k, groups)
+                value = value + q_recv[j, src, :, col : col + HEAD_DIM].astype(jnp.float32)
+            return value * scale
+
+        for h in range(kv_heads):
+            fresh = pl.ds(pl.multiple_of(kept + row, STRETCH), STRETCH)
+            key_new = rotate(total(q_cols + h * HEAD_DIM), cosine, sine).astype(jnp.bfloat16)
+            k_all[h, fresh, :HEAD_DIM] = key_new
+            k_all[h, fresh, HEAD_DIM:] = key_new
+            v_all[h, fresh, :] = total(q_cols + kv_cols + h * HEAD_DIM).astype(jnp.bfloat16)
+        for h in range(head_total):
+            query = rotate(total(h * HEAD_DIM), cosine, sine) * HEAD_DIM ** (-0.5)
+            high = query.astype(jnp.bfloat16)
+            q_cat[h, :, :HEAD_DIM] = high
+            q_cat[h, :, HEAD_DIM:] = (query - high.astype(jnp.float32)).astype(jnp.bfloat16)
+
+        for h in range(kv_heads):
+            for i in range(group_size):
+                n = h * group_size + i
+                scores = lax.dot_general(
+                    q_cat[n], k_all[h], (((1,), (1,)), ((), ())), preferred_element_type=jnp.float32
+                ) + bias_ref[pl.ds(row, STRETCH), :]
+                probs = jnp.exp(scores - jnp.max(scores, axis=1, keepdims=True))
+                norm = jnp.sum(probs, axis=1, keepdims=True)
+                mixed = jnp.dot(
+                    probs.astype(jnp.bfloat16), v_all[h], preferred_element_type=jnp.float32
+                )
+                heads[j, g, :, n * HEAD_DIM : (n + 1) * HEAD_DIM] = (mixed / norm).astype(jnp.bfloat16)
+            for k in range(1, groups):
+                h_copy(j, h, g, lax.rem(g + k, groups)).start()
+
+        order = (0, 1, 3, 2) if groups == 4 else range(groups)
+        for k in order:
+            tr = lax.rem(g + k, groups)
+            if k:
+                for h in range(kv_heads):
+                    h_copy(j, h, tr, tr).wait_recv()
+            p_send[j, tr] = jnp.dot(
+                heads[j, tr], w_out[...], preferred_element_type=jnp.float32
+            ).astype(jnp.bfloat16)
+            p_copy(j, tr).start()
+        for k in order:
+            tr = lax.rem(g + k, groups)
+            p_copy(j, tr).wait_recv()
+            attn = p_send[j, tr].astype(jnp.float32) + p_recv[j, tr].astype(jnp.float32)
+            x_next[j, tr] = (xbuf[j, tr].astype(jnp.float32) + attn).astype(jnp.bfloat16)
+
+            @pl.when(s < last)
+            def _():
+                x_copy(j, tr, s + 1).start()
+
+            a_send[j, tr] = attn.astype(jnp.bfloat16)
+
+            @pl.when(g // per_t == t)
+            def _():
+                if k:
+                    a_copy(j, tr, lax.rem(g, per_t), tr).start()
+
+    @pl.loop(0, slots)
+    def _(j):
+        rows = pl.ds(pl.multiple_of(j * STRETCH, STRETCH), STRETCH)
+
+        @pl.when(s > 0)
+        def _():
+            hc_copy(j, s).wait_recv()
+
+        for c in range(per_t):
+            cols = slice(c * width, (c + 1) * width)
+            owner = per_t * t + c
+
+            @pl.when(owner != g)
+            def _():
+                a_copy(j, g, c, owner).wait_recv()
+                attn_ref[rows, cols] = a_recv[j, c]
+
+            @pl.when(owner == g)
+            def _():
+                attn_ref[rows, cols] = a_send[j, g]
+
+            @pl.when(s == 0)
+            def _():
+                h_send[j, :, cols] = (
+                    x_in[rows, cols].astype(jnp.float32) + attn_ref[rows, cols].astype(jnp.float32)
+                ).astype(jnp.bfloat16)
+
+            @pl.when(s > 0)
+            def _():
+                h_send[j, :, cols] = (
+                    h_recv[j, :, cols].astype(jnp.float32)
+                    + attn_ref[rows, cols].astype(jnp.float32)
+                ).astype(jnp.bfloat16)
+
+        @pl.when(s < last)
+        def _():
+            hc_copy(j, s + 1).start()
+
+        hid_ref[rows, :] = h_send[j]
+
+    for_inputs(lambda copy: copy.wait_send())
+
+    @pl.loop(0, slots)
+    def _(j):
+        for k in range(groups):
+            tr = lax.rem(g + k, groups)
+            if k:
+                q_copy(j, tr, g, g, dev(s, tr, t)).wait_send()
+                ss_copy(j, tr, g, g, dev(s, tr, t)).wait_send()
+                for h in range(kv_heads):
+                    h_copy(j, h, g, tr).wait_send()
+
+                @pl.when(g // per_t == t)
+                def _():
+                    a_copy(j, tr, lax.rem(g, per_t), tr).wait_send()
+
+            p_copy(j, tr).wait_send()
+
+            @pl.when(s < last)
+            def _():
+                x_copy(j, tr, s + 1).wait_send()
+
+        @pl.when(s < last)
+        def _():
+            hc_copy(j, s + 1).wait_send()
+
+
+def relay_shards(hidden_in, kv_cache, norm_gain, w_query, w_keyval, w_out, stretch_count, prefix_len):
+    sections = lax.axis_size("section")
+    groups = lax.axis_size("dp")
+    tensors = lax.axis_size("tensor")
+    width = w_query.shape[1]
+    q_cols = w_query.shape[2]
+    kv_store = kv_cache[0, 0]
+    kept, kv_cols = kv_store.shape[1:]
+    kv_heads = kv_cols // HEAD_DIM
+    head_total = q_cols // HEAD_DIM
+    rows_all = hidden_in.shape[0]
+    slots = rows_all // STRETCH
+    out_cols = hidden_in.shape[1]
+    all_cols = q_cols + 2 * kv_cols
+    per_t = groups // tensors
+    gain = lax.dynamic_slice_in_dim(norm_gain, lax.axis_index("dp") * width, width, 1)
+    prefix = prefix_len[0]
+    row_idx = jnp.arange(rows_all, dtype=jnp.int32)
+    half_dim = HEAD_DIM // 2
+    inv_freq = theta_base ** (-(jnp.arange(half_dim, dtype=jnp.float32) * 2.0 / HEAD_DIM))
+    angles = (prefix + row_idx).astype(jnp.float32)[:, None] * inv_freq[None, :]
+    cosine, sine = jnp.cos(angles), jnp.sin(angles)
+    cos_full = jnp.concatenate([cosine, cosine], axis=1)
+    sin_full = jnp.concatenate([-sine, sine], axis=1)
+    key_idx = jnp.arange(kept + rows_all, dtype=jnp.int32)[None, :]
+    visible = jnp.where(key_idx < kept, key_idx < prefix, key_idx - kept <= row_idx[:, None])
+    bias = jnp.where(visible, 0.0, masked_score).astype(jnp.float32)
+    vmem = pl.BlockSpec(memory_space=pltpu.VMEM)
+    bf16 = jnp.bfloat16
+    dma = pltpu.SemaphoreType.DMA
+    block = (slots, groups, STRETCH)
+    attn, hid = pl.pallas_call(
+        functools.partial(relay_kernel, slots, sections, groups, tensors),
+        out_shape=[jax.ShapeDtypeStruct((rows_all, out_cols), bf16)] * 2,
+        in_specs=[vmem] * 9,
+        out_specs=[vmem] * 2,
+        scratch_shapes=[
+            pltpu.VMEM(block + (width,), bf16),
+            pltpu.VMEM(block + (all_cols,), bf16),
+            pltpu.VMEM(block + (all_cols,), bf16),
+            pltpu.VMEM(block + (HEAD_DIM,), jnp.float32),
+            pltpu.VMEM(block + (HEAD_DIM,), jnp.float32),
+            pltpu.VMEM((STRETCH, all_cols), jnp.float32),
+            pltpu.VMEM((head_total, STRETCH, 2 * HEAD_DIM), bf16),
+            pltpu.VMEM((kv_heads, kept + rows_all, 2 * HEAD_DIM), bf16),
+            pltpu.VMEM((kv_heads, kept + rows_all, HEAD_DIM), bf16),
+            pltpu.VMEM(block + (q_cols,), bf16),
+            pltpu.VMEM(block + (width,), bf16),
+            pltpu.VMEM(block + (width,), bf16),
+            pltpu.VMEM(block + (width,), bf16),
+            pltpu.VMEM(block + (width,), bf16),
+            pltpu.VMEM((slots, per_t, STRETCH, width), bf16),
+            pltpu.VMEM((slots, STRETCH, out_cols), bf16),
+            pltpu.VMEM((slots, STRETCH, out_cols), bf16),
+            dma((slots, per_t, tensors)),
+            dma((slots, groups)),
+            dma((slots, groups)),
+            dma((slots, groups)),
+            dma((slots, groups)),
+            dma((slots, groups)),
+            dma((slots, groups, kv_heads)),
+            dma((slots, groups, kv_heads)),
+            dma((slots, groups)),
+            dma((slots, groups)),
+            dma((slots, groups)),
+            dma((slots, groups)),
+            dma((slots, per_t)),
+            dma((slots,)),
+            dma((slots,)),
+            dma((slots,)),
+        ],
+        compiler_params=pltpu.CompilerParams(
+            collective_id=0, has_side_effects=True, vmem_limit_bytes=60 * 2**20
+        ),
+    )(
+        hidden_in, w_query[0], w_keyval[0].reshape(width, 2 * kv_cols), w_out[0],
+        gain, kv_store, cos_full, sin_full, bias,
+    )
+    live = (row_idx // STRETCH < stretch_count[0])[:, None]
+    return (
+        jnp.where(live, attn, jnp.zeros_like(attn))[None],
+        jnp.where(live, hid, jnp.zeros_like(hid))[None],
+    )
+
+
+def relay_fits(mesh, width, model_cols):
+    return mesh.shape["tensor"] == 2 and width % HEAD_DIM == 0 and model_cols % width == 0
+
+
 def solution(mesh):
+    def either(hidden_in, kv_cache, norm_gain, w_query, *rest):
+        fits = relay_fits(mesh, w_query.shape[1], hidden_in.shape[1])
+        body = relay_shards if fits else shards
+        return body(hidden_in, kv_cache, norm_gain, w_query, *rest)
+
     return jax.shard_map(
-        shards,
+        either,
         mesh=mesh,
         in_specs=(
             P("dp", "tensor"),

time: 1130 us -> 471 us (0.42); the launches traced: 1120 us -> 471 us
  waiting for transfers between devices: 805 us -> 0 us
  Pallas kernels: 0 us -> 461 us
  matrix products: 170 us -> 0 us
  other arithmetic: 62.4 us -> 6.13 us
  local copies, waits for them, and re-layouts: 54.7 us -> 1.97 us
  between operations: 17.4 us -> 2.08 us
    all_gather x8 -> x0, waiting for transfers between devices: 626 us -> none  [the longest x1 220 us: shards(): lax.all_gather(w_query, 'dp', axis=1, tiled=True)]
    pallas_call x0 -> x1, Pallas kernels: none -> 461 us  [relay_shards(): pl.pallas_call(functools.partial(relay_kernel, slots, sections, groups, t...]
    dot_general x55 -> x0, matrix products: 170 us -> none  [the longest x5 38.5 us: shards(): partials = jnp.dot(mixed_heads, out_w, preferred_element_type=jnp.float32)]
    reduce_scatter x5 -> x0, waiting for transfers between devices: 163 us -> none  [shards(): lax.psum_scatter(partials.astype(jnp.bfloat16), 'tensor', scatter_dimensi...]
    dot_general x1 -> x0, local copies, waits for them, and re-layouts: 18.3 us -> none  [shards(): jnp.dot(normed, query_w, preferred_element_type=jnp.float32)]
    lt x20 -> x2, other arithmetic: 18.2 us -> 0.01 us  [the longest x1 0.01 us: relay_shards(): live = (row_idx // STRETCH < stretch_count[0])[:, None]]
    reduce_sum x20 -> x0, other arithmetic: 17.5 us -> none  [the longest x5 10.4 us: shards(): jnp.mean(x_float * x_float, axis=1, keepdims=True) + eps_norm]
    unnamed x144 -> x5, local copies, waits for them, and re-layouts: 16.2 us -> 1.37 us
  transfers between devices with their start and end apart: 17 -> 0, of which waited for: 17 -> 0; matrix products, arithmetic and copies ran while one was open for 6% -> 0% of each run, Pallas kernels for 0% -> 0%
where the time goes in v1:
time: 471 us
  Pallas kernels  461 us (98%)
  other arithmetic  6.13 us (1%)
    pallas_call x1, Pallas kernels, relay_shards(): pl.pallas_call(functools.partial(relay_kernel, slots, sections, groups, t...  461 us

profile of v1, /device:TPU:7, one launch (start us, length us, event | category | flops | bytes accessed | tf_op | source)
XLA Modules:
  0.0 471.2 jit_solution(14460278015224372425)
XLA Ops:
  0.6 0.0 copy-start
  0.6 0.0 copy-start.1
  1.4 0.5 fusion.2
  2.0 0.8 pad_maximum_fusion
  2.8 0.0 copy-done
  2.8 0.6 constant_dynamic-slice_fusion.gain
  3.4 1.3 fusion.1.bias_ref
  4.7 0.0 copy-done.1
  4.7 1.4 copy.10
  6.1 461.0 %shard_map.95 = (bf16[256,2560]{1,0:T(8,128)(2,1)}, bf16[256,2560]{1,0:T(8,128)(2,1)}) custom-call(bf16[256,2560]{1,0:T(8,128)(2,1)} %x_in.1, bf16[1280,1280]{1,0:T(8,128)(2,1)} %bitcast.16, bf16[1280,512]{1,0:T(8,128)(2,1)} %bitcast.15, bf16[1280,1280]{1,0:T(8,128)(2,1)} %bitcast.17, f32[1,1280]{1,0:T(1,128)} %constant_dynamic-slice_fusion.gain, ...), custom_call_target="tpu_custom_call" | custom-call | tf_op jit(solution)/shard_map/pallas_call | solution.py:525
  467.8 3.4 select_bitcast_fusion
  (5 shorter events, 0.0 us)
Async XLA Ops:
  0.6 2.2 copy-start
  0.6 4.1 copy-start.1

commit v2 on v1

--- a/solution.py
+++ b/solution.py
@@ -215,6 +215,7 @@
     group_size = head_total // kv_heads
     kept = kv.shape[1]
     half_cols = group_size * HEAD_DIM
+    order = tuple(k for k in range(groups) if k != 2) + (2,) if groups > 2 else tuple(range(groups))
 
     def dev(sec, grp, ten):
         return {"section": sec, "dp": grp, "tensor": ten}
@@ -331,7 +332,7 @@
     @pl.loop(0, slots)
     def _(j):
         row = pl.multiple_of(j * STRETCH, STRETCH)
-        for k in (2, 1, 3, 0) if groups == 4 else list(range(1, groups)) + [0]:
+        for k in order:
             d = lax.rem(g + k, groups)
             arrives = jnp.logical_not(is_local) | (d != g)
 
@@ -397,17 +398,19 @@
             for k in range(1, groups):
                 h_copy(j, h, g, lax.rem(g + k, groups)).start()
 
-        order = (0, 1, 3, 2) if groups == 4 else range(groups)
-        for k in order:
-            tr = lax.rem(g + k, groups)
-            if k:
-                for h in range(kv_heads):
-                    h_copy(j, h, tr, tr).wait_recv()
-            p_send[j, tr] = jnp.dot(
-                heads[j, tr], w_out[...], preferred_element_type=jnp.float32
-            ).astype(jnp.bfloat16)
-            p_copy(j, tr).start()
-        for k in order:
+        for step, k in enumerate(order + (None,)):
+            if k is not None:
+                tr = lax.rem(g + k, groups)
+                if k:
+                    for h in range(kv_heads):
+                        h_copy(j, h, tr, tr).wait_recv()
+                p_send[j, tr] = jnp.dot(
+                    heads[j, tr], w_out[...], preferred_element_type=jnp.float32
+                ).astype(jnp.bfloat16)
+                p_copy(j, tr).start()
+            if step == 0:
+                continue
+            k = order[step - 1]
             tr = lax.rem(g + k, groups)
             p_copy(j, tr).wait_recv()
             attn = p_send[j, tr].astype(jnp.float32) + p_recv[j, tr].astype(jnp.float32)

time: 471 us -> 463 us (0.983)
  Pallas kernels: 461 us -> 453 us
    pallas_call x1, Pallas kernels: 461 us -> 453 us  [relay_shards(): pl.pallas_call(functools.partial(relay_kernel, slots, sections, groups, t...]
where the time goes in v2:
time: 463 us
  Pallas kernels  453 us (98%)
  other arithmetic  6.13 us (1%)
    pallas_call x1, Pallas kernels, relay_shards(): pl.pallas_call(functools.partial(relay_kernel, slots, sections, groups, t...  453 us

profile of v2, /device:TPU:7, one launch (start us, length us, event | category | flops | bytes accessed | tf_op | source)
XLA Modules:
  0.0 463.0 jit_solution(17415530414995816961)
XLA Ops:
  0.6 0.0 copy-start
  0.6 0.0 copy-start.1
  1.4 0.5 fusion.2
  2.0 0.8 pad_maximum_fusion
  2.8 0.0 copy-done
  2.8 0.6 constant_dynamic-slice_fusion.gain
  3.4 1.3 fusion.1.bias_ref
  4.7 0.0 copy-done.1
  4.7 1.4 copy.10
  6.1 452.8 %shard_map.95 = (bf16[256,2560]{1,0:T(8,128)(2,1)}, bf16[256,2560]{1,0:T(8,128)(2,1)}) custom-call(bf16[256,2560]{1,0:T(8,128)(2,1)} %x_in.1, bf16[1280,1280]{1,0:T(8,128)(2,1)} %bitcast.16, bf16[1280,512]{1,0:T(8,128)(2,1)} %bitcast.15, bf16[1280,1280]{1,0:T(8,128)(2,1)} %bitcast.17, f32[1,1280]{1,0:T(1,128)} %constant_dynamic-slice_fusion.gain, ...), custom_call_target="tpu_custom_call" | custom-call | tf_op jit(solution)/shard_map/pallas_call | solution.py:528
  459.6 3.4 select_bitcast_fusion
  (5 shorter events, 0.0 us)
Async XLA Ops:
  0.6 2.2 copy-start
  0.6 4.1 copy-start.1
